TPU v7x, 512 devices: a whole 4x8x8 slice. The times are simulated.
512 devices in a mesh: row: 32 (over x, y), col: 16 (over z, core).
Axes of the slice: x: 4, y: 8, z: 8, core: 2. Of those that a mesh axis runs over, the one named last changes fastest.
Arguments:
- hessian: float32 [2, 8192, 4, 4096], P(None, 'row', None, 'col'), as said below
Outputs:
- factored: float32 [2, 8192, 4, 4096], P(None, 'row', None, 'col')
Inputs may be any that keep to these rules, and one draw needn't show every extreme that they name: hessian, read as the 16384 x 16384 matrix H0, is symmetric and positive definite.
All inputs are finite; a program needn't handle non-finite values.
Results may differ from a plain program's by a relative error of at most 0.0003.
Values sent between devices are 32-bit elements; how exact they have to be, the bound alone decides.
A program may use at most 64 MiB of HBM per device.

v0:
```python
import jax
import jax.numpy as jnp
from jax import lax
from jax.sharding import PartitionSpec as P


def broadcast(x, axis, root):
    mine = lax.axis_index(axis) == root
    return lax.psum(jnp.where(mine, x, jnp.zeros_like(x)), axis)


def invert_factor(diagonal):
    lower_factor = jnp.linalg.cholesky(diagonal)
    identity = jnp.eye(diagonal.shape[0], dtype=diagonal.dtype)
    return lax.linalg.triangular_solve(lower_factor, identity, left_side=True, lower=True)


def outer_update(own_panel, across):
    row_cycles, block_width, depth = own_panel.shape
    column_count = across.shape[0]
    product_flat = jnp.dot(
        own_panel.reshape(row_cycles * block_width, depth),
        across.reshape(column_count * block_width, depth).T,
        precision=lax.Precision.HIGHEST,
    )
    return product_flat.reshape(row_cycles, block_width, column_count, block_width)


def on_device(hessian):
    row_count = lax.axis_size("row")
    column_count = lax.axis_size("col")
    row_index = lax.axis_index("row")
    column_index = lax.axis_index("col")
    row_cycles, block_width, column_cycles, _ = hessian.shape
    row_blocks = row_index + row_count * jnp.arange(row_cycles, dtype=jnp.int32)
    col_blocks = column_index + column_count * jnp.arange(column_cycles, dtype=jnp.int32)
    offsets = jnp.arange(block_width, dtype=jnp.int32)
    row_position = row_blocks[:, None] * block_width + offsets[None, :]

    def apply_factor(column, inverse, panel_index):
        own_panel = jnp.dot(
            column.reshape(row_cycles * block_width, block_width),
            inverse.T,
            precision=lax.Precision.HIGHEST,
        )
        own_panel = own_panel.reshape(row_cycles, block_width, block_width)
        keep_mask = row_position[:, :, None] >= panel_index * block_width + offsets[None, None, :]
        return jnp.where(keep_mask, own_panel, jnp.zeros_like(own_panel))

    def spread_rows(own_panel):
        depth = own_panel.shape[2]
        pieces = []
        for root_half in range(2):
            pieces.append(broadcast(own_panel, "row", column_index + root_half * column_count))
        across = jnp.stack(pieces, axis=1)
        return across.reshape(column_cycles, block_width, depth)

    def make_panel(matrix, panel_index):
        column_slab = matrix[:, :, panel_index // column_count, :]
        column = broadcast(column_slab, "col", panel_index % column_count)
        diagonal = broadcast(column[panel_index // row_count], "row", panel_index % row_count)
        inverse = invert_factor(diagonal)
        own_panel = apply_factor(column, inverse, panel_index)
        return (own_panel, spread_rows(own_panel))

    matrix = hessian
    first_panel, first_across = make_panel(matrix, 0)
    matrix = matrix - outer_update(first_panel, first_across)
    second_panel, second_across = make_panel(matrix, 1)
    matrix = matrix - outer_update(second_panel, second_across)
    row_global = row_blocks[:, None, None, None]
    col_global = col_blocks[None, None, :, None]
    result = jnp.where(row_global < 2, jnp.zeros_like(matrix), matrix)
    result = jnp.where(col_global == 0, first_panel[:, :, None, :], result)
    result = jnp.where(col_global == 1, second_panel[:, :, None, :], result)
    return result


def solution(mesh):
    in_specs = (P(None, "row", None, "col"),)
    out_specs = P(None, "row", None, "col")
    return jax.shard_map(
        on_device, mesh=mesh, in_specs=in_specs, out_specs=out_specs, check_vma=False
    )
```

profile of v0, /device:TPU:64, one launch (start us, length us, event | category | flops | bytes accessed | tf_op | source)
XLA Modules:
  0.0 1026.2 jit_solution(2998131894410887725)
XLA Ops:
  6.5 1.9 copy.17
  8.5 0.8 fusion.1
  9.4 117.4 %all-reduce.10.cloned.1.call-done = f32[2,256,256]{1,2,0:T(8,128)} async-done(((f32[2,256,256]{1,2,0:T(8,128)}), f32[2,256,256]{1,2,0:T(8,128)}) %all-reduce.10.cloned.1.call-update) | async-done | bytes 524304 | tf_op jit(solution)/shard_map/psum | solution.py:9
  126.8 1.7 fusion.5
  128.6 0.1 iota_add_fusion
  128.7 159.6 %all-reduce.12.cloned.1.call-done = f32[256,256]{0,1:T(8,128)} async-done(((f32[256,256]{0,1:T(8,128)}), f32[256,256]{0,1:T(8,128)}) %all-reduce.12.cloned.1.call-update) | async-done | bytes 262160 | tf_op jit(solution)/shard_map/psum | solution.py:9
  288.2 1.1 copy.14
  289.3 1.0 fusion.11
  290.4 11.7 %cholesky.130 = f32[128,128]{1,0:T(8,128)S(1)} custom-call(f32[128,128]{1,0:T(8,128)S(1)} %cholesky.194), custom_call_target="Cholesky" | custom-call | tf_op jit(solution)/shard_map/jit(cholesky)/cholesky | solution.py:13
  302.1 9.8 custom-call.13
  311.9 1.0 constant_dynamic-update-slice_fusion.3
  313.0 1.1 convolution_subtract_fusion.4
  314.1 11.7 %cholesky.147 = f32[128,128]{1,0:T(8,128)S(1)} custom-call(f32[128,128]{1,0:T(8,128)S(1)} %convolution_subtract_fusion.4), custom_call_target="Cholesky" | custom-call | tf_op jit(solution)/shard_map/jit(cholesky)/cholesky | solution.py:13
  325.9 0.6 compare_reduce_fusion.2
  327.8 0.1 broadcast.208
  327.8 4.0 while.4
  328.1 0.6 fusion.49
  328.6 1.3 bitcast_dynamic-update-slice_fusion.4
  330.0 0.6 fusion.49
  330.6 1.3 bitcast_dynamic-update-slice_fusion.4
  331.9 19.7 %custom-call.14 = f32[2,128,128]{1,2,0:T(8,128)S(1)} custom-call(f32[2,128,128]{2,1,0:T(8,128)S(1)} %get-tuple-element.21), custom_call_target="InvertDiagBlocksLowerTriangular" | custom-call | tf_op jit(solution)/shard_map/triangular_solve/custom-call.0 | solution.py:15
  351.6 0.3 fusion.15
  351.9 0.3 convolution_subtract_fusion.2
  352.1 0.3 fusion.22
  352.5 1.0 convolution_select_fusion.1
  353.5 1.1 select_bitcast_fusion.3
  354.6 158.0 %all-reduce.20.cloned.1.call-done = (f32[2,1,256,256]{3,2,0,1:T(8,128)}, f32[2,1,256,256]{3,2,0,1:T(8,128)}) async-done(((f32[2,1,256,256]{3,2,0,1:T(8,128)}, f32[2,1,256,256]{3,2,0,1:T(8,128)}), (f32[2,1,256,256]{3,2,0,1:T(8,128)}, f32[2,1,256,256]{3,2,0,1:T(8,128)})) %all-reduce.20.cloned.1.call-update) | async-done | bytes 1048592 | tf_op jit(solution)/shard_map/psum | solution.py:9
  512.6 1.3 pad_maximum_fusion
  513.9 0.1 copy.16
  514.0 2.0 convolution_subtract_fusion
  515.9 1.3 copy-done
  517.3 0.8 fusion
  518.2 110.9 %all-reduce.14.cloned.1.call-done = f32[2,256,256]{1,2,0:T(8,128)} async-done(((f32[2,256,256]{1,2,0:T(8,128)}), f32[2,256,256]{1,2,0:T(8,128)}) %all-reduce.14.cloned.1.call-update) | async-done | bytes 524304 | tf_op jit(solution)/shard_map/psum | solution.py:9
  629.0 1.7 fusion.4
  630.8 159.1 %all-reduce.16.cloned.1.call-done = f32[256,256]{0,1:T(8,128)} async-done(((f32[256,256]{0,1:T(8,128)}), f32[256,256]{0,1:T(8,128)}) %all-reduce.16.cloned.1.call-update) | async-done | bytes 262160 | tf_op jit(solution)/shard_map/psum | solution.py:9
  789.9 1.1 copy.19
  791.0 1.0 fusion.10
  792.0 11.7 %cholesky.164 = f32[128,128]{1,0:T(8,128)S(1)} custom-call(f32[128,128]{1,0:T(8,128)S(1)} %cholesky.197), custom_call_target="Cholesky" | custom-call | tf_op jit(solution)/shard_map/jit(cholesky)/cholesky | solution.py:13
  803.8 9.8 custom-call.15
  813.6 0.2 constant_dynamic-update-slice_fusion.1
  813.8 0.3 convolution_subtract_fusion.3
  814.1 11.7 %cholesky.181 = f32[128,128]{1,0:T(8,128)S(1)} custom-call(f32[128,128]{1,0:T(8,128)S(1)} %convolution_subtract_fusion.3), custom_call_target="Cholesky" | custom-call | tf_op jit(solution)/shard_map/jit(cholesky)/cholesky | solution.py:13
  825.8 0.7 compare_reduce_fusion
  826.5 0.6 compare_reduce_fusion.1
  828.4 4.0 while.5
  828.7 0.6 fusion.50
  829.3 1.3 bitcast_dynamic-update-slice_fusion.5
  830.6 0.6 fusion.50
  831.2 1.3 bitcast_dynamic-update-slice_fusion.5
  832.5 19.7 %custom-call.16 = f32[2,128,128]{1,2,0:T(8,128)S(1)} custom-call(f32[2,128,128]{2,1,0:T(8,128)S(1)} %get-tuple-element.22), custom_call_target="InvertDiagBlocksLowerTriangular" | custom-call | tf_op jit(solution)/shard_map/triangular_solve/custom-call.0 | solution.py:15
  852.2 0.3 fusion.13
  852.5 0.3 convolution_subtract_fusion.1
  852.7 0.3 fusion.18
  853.1 1.0 convolution_select_fusion
  854.1 1.1 select_bitcast_fusion.1
  855.2 1.0 copy.22
  856.2 0.2 copy.21
  856.4 156.8 %all-reduce.18.cloned.1.call-done = (f32[2,1,256,256]{3,2,0,1:T(8,128)}, f32[2,1,256,256]{3,2,0,1:T(8,128)}) async-done(((f32[2,1,256,256]{3,2,0,1:T(8,128)}, f32[2,1,256,256]{3,2,0,1:T(8,128)}), (f32[2,1,256,256]{3,2,0,1:T(8,128)}, f32[2,1,256,256]{3,2,0,1:T(8,128)})) %all-reduce.18.cloned.1.call-update) | async-done | bytes 1048592 | tf_op jit(solution)/shard_map/psum | solution.py:9
  1013.3 1.4 pad_maximum_fusion.1
  1014.7 0.1 copy.23
  1014.8 0.4 copy-done.1
  1015.2 0.1 copy-done.2
  1015.3 2.3 select_select_fusion
  1017.6 1.8 copy.25
  (43 shorter events, 0.7 us)
Async XLA Ops:
  6.5 120.3 %all-reduce.10.cloned.1.call-start = ((), (), s32[]{:S(2)}) async-start(), calls=%async_computation | async-start | bytes 1048576 | tf_op jit(solution)/shard_map/psum | solution.py:9
  9.3 278.9 %all-reduce.12.cloned.1.call-start = ((), (), s32[]{:S(2)}) async-start(), calls=%async_computation.1 | async-start | bytes 524288 | tf_op jit(solution)/shard_map/psum | solution.py:9
  128.5 384.1 %all-reduce.20.cloned.1.call-start = ((), (), s32[]{:S(2)}) async-start(), calls=%async_computation.5 | async-start | bytes 2097152 | tf_op jit(solution)/shard_map/psum | solution.py:9
  290.3 11.8 %copy-start.5 = (f32[256,256]{1,0:T(8,128)}, f32[256,256]{1,0:T(8,128)S(1)}, u32[]{:S(2)}) copy-start(f32[256,256]{1,0:T(8,128)S(1)} %fusion.11) | copy-start | bytes 786436
  290.3 62.1 %copy-start.3 = (f32[2,256,256]{1,2,0:T(8,128)S(1)}, f32[2,256,256]{1,2,0:T(8,128)}, u32[]{:S(2)}) copy-start(f32[2,256,256]{1,2,0:T(8,128)} %all-reduce.10.cloned.1.call-done) | copy-start | bytes 1572868
  354.6 274.5 %all-reduce.14.cloned.1.call-start = ((), (), s32[]{:S(2)}) async-start(), calls=%async_computation.2 | async-start | bytes 1048576 | tf_op jit(solution)/shard_map/psum | solution.py:9
  515.9 1.3 copy-start
  518.1 271.8 %all-reduce.16.cloned.1.call-start = ((), (), s32[]{:S(2)}) async-start(), calls=%async_computation.3 | async-start | bytes 524288 | tf_op jit(solution)/shard_map/psum | solution.py:9
  630.7 382.5 %all-reduce.18.cloned.1.call-start = ((), (), s32[]{:S(2)}) async-start(), calls=%async_computation.4 | async-start | bytes 2097152 | tf_op jit(solution)/shard_map/psum | solution.py:9
  792.0 61.1 %copy-start.4 = (f32[2,256,256]{1,2,0:T(8,128)S(1)}, f32[2,256,256]{1,2,0:T(8,128)}, u32[]{:S(2)}) copy-start(f32[2,256,256]{1,2,0:T(8,128)} %all-reduce.14.cloned.1.call-done) | copy-start | bytes 1572868
  1013.3 1.9 copy-start.1
  1013.3 2.0 copy-start.2
Sparse Core Ops, SparseCore 0:
  9.7 117.1 all-reduce.9
  130.7 157.5 all-reduce.11
  354.7 157.8 all-reduce.19
  518.2 110.7 all-reduce.13
  632.3 157.5 all-reduce.15
  855.3 157.8 all-reduce.17
where the time goes:
time: 1030 us
  waiting for transfers between devices  862 us (84%)
  other arithmetic  120 us (12%)
  local copies, waits for them, and re-layouts  16.7 us (2%)
  between operations  16.3 us (2%)
  matrix products  10.7 us (1%)
    psum x6, waiting for transfers between devices, broadcast(): return lax.psum(jnp.where(mine, x, jnp.zeros_like(x)), axis)  862 us
    another operation x13, other arithmetic, invert_factor(): lower_factor = jnp.linalg.cholesky(diagonal)  68.6 us
    another operation x5, other arithmetic, invert_factor(): lax.linalg.triangular_solve(lower_factor, identity, left_side=True, lower...  39.4 us
  transfers between devices with their start and end apart: 6, of which 6 were waited for; matrix products, arithmetic and copies ran while one was open for 0% of the time, Pallas kernels for 0%

commit v1 on v0

--- a/solution.py
+++ b/solution.py
@@ -6,7 +6,7 @@
 
 def broadcast(x, axis, root):
     mine = lax.axis_index(axis) == root
-    return lax.psum(jnp.where(mine, x, jnp.zeros_like(x)), axis)
+    return jnp.sum(lax.all_gather(jnp.where(mine, x, jnp.zeros_like(x)), axis), axis=0)
 
 
 def invert_factor(diagonal):

time: 1030 us -> 1110 us (1.078)
  the two profiles are of different devices: /device:TPU:64 before, /device:TPU:1 now
where the time goes in v1:
time: 1110 us; the launch traced here: 1100 us
  waiting for transfers between devices  890 us (80%)
  other arithmetic  161 us (15%)
  local copies, waits for them, and re-layouts  19.2 us (2%)
  between operations  16.7 us (2%)
  matrix products  13.5 us (1%)
    all_gather x8, waiting for transfers between devices, broadcast(): lax.all_gather(jnp.where(mine, x, jnp.zeros_like(x)), axis)  888 us
    another operation x13, other arithmetic, invert_factor(): lower_factor = jnp.linalg.cholesky(diagonal)  69.3 us
    reduce_sum x8, other arithmetic, broadcast(): jnp.sum(lax.all_gather(jnp.where(mine, x, jnp.zeros_like(x)), axis), axis=0)  44.2 us
    another operation x5, other arithmetic, invert_factor(): lax.linalg.triangular_solve(lower_factor, identity, left_side=True, lower...  41.9 us
  transfers between devices with their start and end apart: 8, of which 8 were waited for; matrix products, arithmetic and copies ran while one was open for 1% of the time, Pallas kernels for 0%

profile of v1, /device:TPU:1, one launch (start us, length us, event | category | flops | bytes accessed | tf_op | source)
XLA Modules:
  0.0 1101.1 jit_solution(2278629708441339545)
XLA Ops:
  6.5 2.0 copy.9
  8.5 0.8 slice_select_fusion.1
  9.5 65.3 %all-gather.19.cloned.1.call-done = f32[32,256,1,256]{3,1,2,0:T(8,128)} async-done(((f32[2,256,1,256]{3,1,2,0:T(8,128)}), f32[32,256,1,256]{3,1,2,0:T(8,128)}) %all-gather.19.cloned.1.call-update) | async-done | bytes 8388624 | tf_op jit(solution)/shard_map/all_gather | solution.py:9
  74.8 4.0 reduce_sum.72
  78.8 0.7 slice_select_fusion.3
  79.7 100.6 %all-gather.15.cloned.1.call-done = f32[32,256,256]{2,1,0:T(8,128)} async-done(((f32[1,256,256]{2,1,0:T(8,128)}), f32[32,256,256]{2,1,0:T(8,128)}) %all-gather.15.cloned.1.call-update) | async-done | bytes 8388624 | tf_op jit(solution)/shard_map/all_gather | solution.py:9
  180.3 3.9 reduce_sum.73
  184.4 11.7 %cholesky.130 = f32[128,128]{1,0:T(8,128)S(1)} custom-call(f32[128,128]{1,0:T(8,128)S(1)} %cholesky.194), custom_call_target="Cholesky" | custom-call | tf_op jit(solution)/shard_map/jit(cholesky)/cholesky | solution.py:13
  196.2 9.8 custom-call.13
  206.5 11.7 %cholesky.147 = f32[128,128]{1,0:T(8,128)S(1)} custom-call(f32[128,128]{1,0:T(8,128)S(1)} %convolution_subtract_fusion.4), custom_call_target="Cholesky" | custom-call | tf_op jit(solution)/shard_map/jit(cholesky)/cholesky | solution.py:13
  218.2 0.7 compare_reduce_fusion.2
  220.4 4.6 while.4
  220.9 0.6 fusion.45
  221.5 1.4 bitcast_dynamic-update-slice_fusion.4
  223.0 0.6 fusion.45
  223.6 1.4 bitcast_dynamic-update-slice_fusion.4
  225.0 19.7 %custom-call.14 = f32[2,128,128]{1,2,0:T(8,128)S(1)} custom-call(f32[2,128,128]{2,1,0:T(8,128)S(1)} %get-tuple-element.21), custom_call_target="InvertDiagBlocksLowerTriangular" | custom-call | tf_op jit(solution)/shard_map/triangular_solve/custom-call.0 | solution.py:15
  245.3 0.3 fusion.18
  245.6 1.6 broadcast_select_fusion.3
  247.3 0.5 all-gather.23.cloned.1.call-update
  247.9 142.8 %all-gather.21.cloned.1.call-done = f32[64,256,256]{2,1,0:T(8,128)} async-done(((f32[2,256,256]{2,1,0:T(8,128)}), f32[64,256,256]{2,1,0:T(8,128)}) %all-gather.21.cloned.1.call-update) | async-done | bytes 16777232 | tf_op jit(solution)/shard_map/all_gather | solution.py:9
  390.6 6.9 reduce_sum.74
  397.5 139.3 %all-gather.23.cloned.1.call-done = f32[64,256,256]{2,1,0:T(8,128)} async-done(((f32[2,256,256]{2,1,0:T(8,128)}), f32[64,256,256]{2,1,0:T(8,128)}) %all-gather.23.cloned.1.call-update) | async-done | bytes 16777232 | tf_op jit(solution)/shard_map/all_gather | solution.py:9
  536.8 6.9 reduce_sum.75
  543.8 1.5 copy-done
  545.3 2.1 convolution_subtract_fusion
  547.5 0.8 slice_select_fusion
  548.4 57.8 %all-gather.25.cloned.1.call-done = f32[32,256,1,256]{3,1,2,0:T(8,128)} async-done(((f32[2,256,1,256]{3,1,2,0:T(8,128)}), f32[32,256,1,256]{3,1,2,0:T(8,128)}) %all-gather.25.cloned.1.call-update) | async-done | bytes 8388624 | tf_op jit(solution)/shard_map/all_gather | solution.py:9
  606.1 4.0 reduce_sum.76
  610.1 0.7 slice_select_fusion.2
  611.1 100.5 %all-gather.17.cloned.1.call-done = f32[32,256,256]{2,1,0:T(8,128)} async-done(((f32[1,256,256]{2,1,0:T(8,128)}), f32[32,256,256]{2,1,0:T(8,128)}) %all-gather.17.cloned.1.call-update) | async-done | bytes 8388624 | tf_op jit(solution)/shard_map/all_gather | solution.py:9
  711.6 3.9 reduce_sum.77
  715.6 0.8 copy.10
  716.4 1.0 fusion.6
  717.4 0.7 copy-done.4
  718.1 11.7 %cholesky.164 = f32[128,128]{1,0:T(8,128)S(1)} custom-call(f32[128,128]{1,0:T(8,128)S(1)} %cholesky.197), custom_call_target="Cholesky" | custom-call | tf_op jit(solution)/shard_map/jit(cholesky)/cholesky | solution.py:13
  729.8 0.7 cholesky.189
  730.6 9.8 custom-call.15
  740.4 1.7 constant_dynamic-update-slice_fusion.1
  742.1 1.1 convolution_subtract_fusion.3
  743.2 11.7 %cholesky.181 = f32[128,128]{1,0:T(8,128)S(1)} custom-call(f32[128,128]{1,0:T(8,128)S(1)} %convolution_subtract_fusion.3), custom_call_target="Cholesky" | custom-call | tf_op jit(solution)/shard_map/jit(cholesky)/cholesky | solution.py:13
  754.9 0.6 select_reduce_fusion
  755.5 0.6 compare_reduce_fusion
  756.2 0.7 compare_reduce_fusion.1
  758.1 1.7 select_select_fusion.1
  759.8 6.0 while.5
  760.1 0.7 fusion.46
  760.7 2.2 bitcast_dynamic-update-slice_fusion.5
  763.0 0.7 fusion.46
  763.7 2.2 bitcast_dynamic-update-slice_fusion.5
  765.9 0.6 copy-done.5
  766.5 20.5 %custom-call.16 = f32[2,128,128]{1,2,0:T(8,128)S(1)} custom-call(f32[2,128,128]{2,1,0:T(8,128)} %copy-done.5), custom_call_target="InvertDiagBlocksLowerTriangular" | custom-call | tf_op jit(solution)/shard_map/triangular_solve/custom-call.0 | solution.py:15
  787.0 0.3 fusion.9
  787.3 1.1 convolution_subtract_fusion.1
  788.4 0.3 fusion.14
  788.8 1.8 broadcast_select_fusion.1
  790.6 0.7 all-gather.29.cloned.1.call-update
  791.3 142.6 %all-gather.27.cloned.1.call-done = f32[64,256,256]{2,1,0:T(8,128)} async-done(((f32[2,256,256]{2,1,0:T(8,128)}), f32[64,256,256]{2,1,0:T(8,128)}) %all-gather.27.cloned.1.call-update) | async-done | bytes 16777232 | tf_op jit(solution)/shard_map/all_gather | solution.py:9
  933.9 6.9 reduce_sum.78
  940.8 139.5 %all-gather.29.cloned.1.call-done = f32[64,256,256]{2,1,0:T(8,128)} async-done(((f32[2,256,256]{2,1,0:T(8,128)}), f32[64,256,256]{2,1,0:T(8,128)}) %all-gather.29.cloned.1.call-update) | async-done | bytes 16777232 | tf_op jit(solution)/shard_map/all_gather | solution.py:9
  1080.3 7.7 reduce_sum.79
  1088.0 1.2 pad_maximum_fusion.1
  1089.2 2.1 select_select_fusion
  1091.3 2.7 copy.11
  (51 shorter events, 2.3 us)
Async XLA Ops:
  6.5 68.3 %all-gather.19.cloned.1.call-start = ((), (), s32[]{:S(2)}) async-start(), calls=%async_computation.2 | async-start | bytes 8912896 | tf_op jit(solution)/shard_map/all_gather | solution.py:9
  9.4 170.9 %all-gather.15.cloned.1.call-start = ((), (), s32[]{:S(2)}) async-start(), calls=%async_computation | async-start | bytes 8650752 | tf_op jit(solution)/shard_map/all_gather | solution.py:9
  79.5 311.1 %all-gather.21.cloned.1.call-start = ((), (), s32[]{:S(2)}) async-start(), calls=%async_computation.3 | async-start | bytes 17301504 | tf_op jit(solution)/shard_map/all_gather | solution.py:9
  79.6 165.4 %copy-start.1 = (f32[256,256]{1,0:T(8,128)}, f32[256,256]{1,0:T(8,128)S(1)}, u32[]{:S(2)}) copy-start(f32[256,256]{1,0:T(8,128)S(1)} %fusion.8) | copy-start | bytes 786436
  247.2 289.6 %all-gather.23.cloned.1.call-start = ((), (), s32[]{:S(2)}) async-start(), calls=%async_computation.4 | async-start | bytes 17301504 | tf_op jit(solution)/shard_map/all_gather | solution.py:9
  247.8 358.3 %all-gather.25.cloned.1.call-start = ((), (), s32[]{:S(2)}) async-start(), calls=%async_computation.5 | async-start | bytes 8912896 | tf_op jit(solution)/shard_map/all_gather | solution.py:9
  543.7 1.6 copy-start
  548.3 163.3 %all-gather.17.cloned.1.call-start = ((), (), s32[]{:S(2)}) async-start(), calls=%async_computation.1 | async-start | bytes 8650752 | tf_op jit(solution)/shard_map/all_gather | solution.py:9
  610.9 323.0 %all-gather.27.cloned.1.call-start = ((), (), s32[]{:S(2)}) async-start(), calls=%async_computation.6 | async-start | bytes 17301504 | tf_op jit(solution)/shard_map/all_gather | solution.py:9
  717.4 0.7 copy-start.4
  718.1 68.9 %copy-start.2 = (f32[256,256]{1,0:T(8,128)S(1)}, f32[256,256]{1,0:T(8,128)}, u32[]{:S(2)}) copy-start(f32[256,256]{1,0:T(8,128)} %copy-done.1) | copy-start | bytes 786436
  765.9 0.6 copy-start.5
  790.5 289.7 %all-gather.29.cloned.1.call-start = ((), (), s32[]{:S(2)}) async-start(), calls=%async_computation.7 | async-start | bytes 17301504 | tf_op jit(solution)/shard_map/all_gather | solution.py:9
  1088.0 1.2 copy-start.3
Sparse Core Ops, SparseCore 0:
  9.5 65.2 all-gather.18
  79.7 100.6 all-gather.14
  247.3 143.2 all-gather.20
  393.6 143.1 all-gather.22
  548.4 57.6 all-gather.24
  611.0 100.6 all-gather.16
  790.7 143.1 all-gather.26
  937.1 143.1 all-gather.28
